TPU v7x, 32 devices: a whole 2x2x4 slice. The times are simulated.
32 devices in a mesh: dp: 2 (over y), row: 4 (over z), col: 4 (over x, core).
Axes of the slice: x: 2, y: 2, z: 4, core: 2. Of those that a mesh axis runs over, the one named last changes fastest.
Arguments:
- hidden_in: bfloat16 [4096, 1600], P(('dp', 'col'), 'row'), may hold values from -6 to 6
- upstream: bfloat16 [4096, 1600], P(('dp', 'col'), 'row')
- segment_ids: int32 [4096], P('dp'), may hold values from 1 to 3, as said below
- qkv_weight: float32 [1600, 4800], P(('row', 'dp'), 'col')
- proj_weight: float32 [1600, 1600], P(('col', 'dp'), 'row'), may hold values from -0.625 to 0.625
- up_weight: float32 [1600, 6400], P(('row', 'dp'), 'col'), may hold values from -0.15625 to 0.15625
- down_weight: float32 [6400, 1600], P(('col', 'dp'), 'row'), may hold values from -0.078125 to 0.078125
- vectors: float32 [8, 1600], replicated
- up_bias: float32 [6400], replicated, may hold values from -3 to 3
- qkv_moments: float32 [2, 1600, 4800], P(None, ('row', 'dp'), 'col'), as said below
- proj_moments: float32 [2, 1600, 1600], P(None, ('col', 'dp'), 'row'), as said below
- up_moments: float32 [2, 1600, 6400], P(None, ('row', 'dp'), 'col'), as said below
- down_moments: float32 [2, 6400, 1600], P(None, ('col', 'dp'), 'row'), as said below
- vector_moments: float32 [2, 8, 1600], replicated, as said below
- bias_moments: float32 [2, 6400], replicated, as said below
Outputs:
- block_out: bfloat16 [4096, 1600], P(('dp', 'col'), 'row')
- input_grad: bfloat16 [4096, 1600], P(('dp', 'col'), 'row')
- qkv_grad: float32 [1600, 4800], P(('row', 'dp'), 'col')
- proj_grad: float32 [1600, 1600], P(('col', 'dp'), 'row')
- up_grad: float32 [1600, 6400], P(('row', 'dp'), 'col')
- down_grad: float32 [6400, 1600], P(('col', 'dp'), 'row')
- vector_grad: float32 [8, 1600], replicated
- bias_grad: float32 [6400], replicated
- new_qkv: float32 [1600, 4800], P(('row', 'dp'), 'col')
- new_proj: float32 [1600, 1600], P(('col', 'dp'), 'row')
- new_up: float32 [1600, 6400], P(('row', 'dp'), 'col')
- new_down: float32 [6400, 1600], P(('col', 'dp'), 'row')
- new_vectors: float32 [8, 1600], replicated
- new_bias: float32 [6400], replicated
- qkv_state: float32 [2, 1600, 4800], P(None, ('row', 'dp'), 'col')
- proj_state: float32 [2, 1600, 1600], P(None, ('col', 'dp'), 'row')
- up_state: float32 [2, 1600, 6400], P(None, ('row', 'dp'), 'col')
- down_state: float32 [2, 6400, 1600], P(None, ('col', 'dp'), 'row')
- vector_state: float32 [2, 8, 1600], replicated
- bias_state: float32 [2, 6400], replicated
Inputs may be any that keep to these rules, and one draw needn't show every extreme that they name: `segment_ids`: ids never fall; a sequence is a run of equal ids; no sequence crosses a multiple of 2048 tokens; the first 2048 tokens form one sequence. `qkv_moments`: the second row is positive. `proj_moments`: the second row is positive. `up_moments`: the second row is positive. `down_moments`: the second row is positive. `vector_moments`: the second row is positive. `bias_moments`: the second row is positive.
All inputs are finite; a program needn't handle non-finite values.
Results may differ from a plain program's by a relative error of at most 0.025.
Values may be sent and summed in bfloat16 or wider, within the bound.
No kernel may reach another device: no remote copies, remote signals or barrier semaphores. Data moves between devices by JAX's collectives and lax.ppermute only.
A program may use at most 256 MiB of HBM per device.

v0:
```python
import math
import jax
import jax.numpy as jnp
from jax import lax
from jax.sharding import PartitionSpec as P

D = 1600
HEADS = 25
HEAD_DIM = 64
HEAD_BLOCK = 5
STEP = 3
EPS_NORM = 1e-05
BETA_ONE = 0.9
BETA_TWO = 0.95
EPS_ADAM = 1e-08
LR_MATRIX = 0.08
LR_VECTOR = 0.3
DECAY = 0.1
NEG_FILL = -1e30
GELU_COEF = 0.7978845608028654
GELU_CUBE = 0.044715


def gelu_tanh(pre_act):
    inside = GELU_COEF * (pre_act + GELU_CUBE * pre_act * pre_act * pre_act)
    return 0.5 * pre_act * (1.0 + jnp.tanh(inside))


def gelu_slope(pre_act):
    inside = GELU_COEF * (pre_act + GELU_CUBE * pre_act * pre_act * pre_act)
    tanh_val = jnp.tanh(inside)
    return 0.5 * (1.0 + tanh_val) + 0.5 * pre_act * (1.0 - tanh_val * tanh_val) * GELU_COEF * (
        1.0 + 3.0 * GELU_CUBE * pre_act * pre_act
    )


def row_totals(first_term, second_term):
    return lax.psum(
        (jnp.sum(first_term, axis=1, keepdims=True), jnp.sum(second_term, axis=1, keepdims=True)),
        "row",
    )


def norm_forward(values, gain_vec, shift_vec):
    row_sums, squares = row_totals(values, values * values)
    center = row_sums / D
    spread = squares / D - center * center
    inverse = lax.rsqrt(spread + EPS_NORM)
    normed = (values - center) * inverse
    return (normed, inverse, (normed * gain_vec + shift_vec).astype(jnp.bfloat16))


def norm_backward(grad_normed, normed, inverse, gain_vec):
    scaled = grad_normed * gain_vec
    first_sum, second_sum = row_totals(scaled, scaled * normed)
    return inverse * (scaled - first_sum / D - normed * (second_sum / D))


def widen(local_rows, weight_block, flipped):
    gathered = lax.all_gather(local_rows, "col", axis=0, tiled=True)
    right_side = weight_block.T if flipped else weight_block
    partial_rows = jnp.dot(gathered, right_side, preferred_element_type=jnp.float32)
    return (
        gathered,
        lax.psum_scatter(
            partial_rows.astype(jnp.bfloat16), "row", scatter_dimension=0, tiled=True
        ).astype(jnp.float32),
    )


def narrow(local_rows, weight_block, flipped):
    gathered = lax.all_gather(local_rows, "row", axis=0, tiled=True)
    right_side = weight_block.T if flipped else weight_block
    partial_rows = jnp.dot(gathered, right_side, preferred_element_type=jnp.float32)
    return (
        gathered,
        lax.psum_scatter(
            partial_rows.astype(jnp.bfloat16), "col", scatter_dimension=0, tiled=True
        ).astype(jnp.float32),
    )


def to_heads(feature_rows):
    return lax.all_to_all(feature_rows, "col", split_axis=0, concat_axis=1, tiled=True)


def from_heads(head_rows):
    return lax.all_to_all(head_rows, "col", split_axis=1, concat_axis=0, tiled=True)


def split_heads(matrix):
    return matrix.reshape(matrix.shape[0], HEADS // HEAD_BLOCK, HEAD_BLOCK, HEAD_DIM).transpose(
        1, 2, 0, 3
    )


def merge_heads(blocks):
    return blocks.transpose(2, 0, 1, 3).reshape(blocks.shape[2], D)


def masked_scores(query_blk, key_blk, allowed):
    scores = jnp.einsum("hqe,hke->hqk", query_blk, key_blk, preferred_element_type=jnp.float32) * (
        1.0 / math.sqrt(HEAD_DIM)
    )
    return jnp.where(allowed[None], scores, NEG_FILL)


def attend(query_blk, key_blk, value_blk, allowed):
    scores = masked_scores(query_blk, key_blk, allowed)
    row_max = jnp.max(scores, axis=2, keepdims=True)
    log_total = row_max + jnp.log(jnp.sum(jnp.exp(scores - row_max), axis=2, keepdims=True))
    chances = jnp.exp(scores - log_total)
    mixed_out = jnp.einsum(
        "hqk,hke->hqe", chances.astype(jnp.bfloat16), value_blk, preferred_element_type=jnp.float32
    )
    return (mixed_out.astype(jnp.bfloat16), log_total)


def query_side(query_blk, key_blk, value_blk, log_total, grad_blk, allowed):
    chances = jnp.exp(masked_scores(query_blk, key_blk, allowed) - log_total)
    grad_chances = jnp.einsum(
        "hqe,hke->hqk", grad_blk, value_blk, preferred_element_type=jnp.float32
    )
    row_dot = jnp.sum(chances * grad_chances, axis=2, keepdims=True)
    grad_scores = (chances * (grad_chances - row_dot)).astype(jnp.bfloat16)
    grad_query = jnp.einsum(
        "hqk,hke->hqe", grad_scores, key_blk, preferred_element_type=jnp.float32
    ) * (1.0 / math.sqrt(HEAD_DIM))
    return (chances, grad_scores, grad_query, row_dot)


def adam_step(weight, gradient, moments, rate):
    first_moment = BETA_ONE * moments[0] + (1.0 - BETA_ONE) * gradient
    second = BETA_TWO * moments[1] + (1.0 - BETA_TWO) * gradient * gradient
    first_fix = 1.0 - BETA_ONE**STEP
    second_fix = 1.0 - BETA_TWO**STEP
    stepped = weight - rate * (
        first_moment / first_fix / (jnp.sqrt(second / second_fix) + EPS_ADAM) + DECAY * weight
    )
    return (stepped, jnp.stack([first_moment, second]))


def per_device(
    hidden_in,
    upstream,
    segment_ids,
    qkv_weight,
    proj_weight,
    up_weight,
    down_weight,
    vectors,
    up_bias,
    qkv_moments,
    proj_moments,
    up_moments,
    down_moments,
    vector_moments,
    bias_moments,
):
    factor = 1.0 / math.sqrt(HEAD_DIM)
    row_index = lax.axis_index("row")
    col_index = lax.axis_index("col")
    row_width = D // lax.axis_size("row")
    qkv_cols = qkv_weight.shape[1]
    up_cols = up_weight.shape[1]
    w_qkv, w_proj, w_up, w_down = (
        lax.all_gather(qkv_weight.astype(jnp.bfloat16), "dp", axis=0, tiled=True),
        lax.all_gather(proj_weight.astype(jnp.bfloat16), "dp", axis=0, tiled=True),
        lax.all_gather(up_weight.astype(jnp.bfloat16), "dp", axis=0, tiled=True),
        lax.all_gather(down_weight.astype(jnp.bfloat16), "dp", axis=0, tiled=True),
    )

    def row_slice(vector_row):
        return lax.dynamic_slice_in_dim(vector_row, row_index * row_width, row_width)

    def place_rows(partial_vec):
        return lax.dynamic_update_slice_in_dim(
            jnp.zeros((D,), jnp.float32), partial_vec, row_index * row_width, 0
        )

    gain_one = row_slice(vectors[0])
    shift_one = row_slice(vectors[1])
    shift_proj = row_slice(vectors[4])
    gain_two = row_slice(vectors[5])
    shift_two = row_slice(vectors[6])
    shift_down = row_slice(vectors[7])
    qkv_full_shift = jnp.concatenate([vectors[2], jnp.zeros((D,), jnp.float32), vectors[3]])
    qkv_shift = lax.dynamic_slice_in_dim(qkv_full_shift, col_index * qkv_cols, qkv_cols)
    up_shift = lax.dynamic_slice_in_dim(up_bias, col_index * up_cols, up_cols)
    inputs_f = hidden_in.astype(jnp.float32)
    normed_one, inverse_one, ln_one = norm_forward(inputs_f, gain_one, shift_one)
    gathered_one, qkv_sum = widen(ln_one, w_qkv, False)
    qkv_rows = (qkv_sum + qkv_shift).astype(jnp.bfloat16)
    qkv_heads = to_heads(qkv_rows)
    query_count = qkv_heads.shape[0]
    group_len = segment_ids.shape[0]
    query_start = (row_index * lax.axis_size("col") + col_index) * query_count
    query_ids = lax.dynamic_slice_in_dim(segment_ids, query_start, query_count)
    query_pos = query_start + jnp.arange(query_count, dtype=jnp.int32)
    key_pos = jnp.arange(group_len, dtype=jnp.int32)
    allowed = (query_ids[:, None] == segment_ids[None, :]) & (
        key_pos[None, :] <= query_pos[:, None]
    )
    key_values = lax.all_gather(qkv_heads[:, D:], ("row", "col"), axis=0, tiled=True)
    query_blocks = split_heads(qkv_heads[:, :D])
    key_blocks = split_heads(key_values[:, :D])
    value_blocks = split_heads(key_values[:, D:])
    attn_blocks, log_totals = lax.map(
        lambda block_items: attend(block_items[0], block_items[1], block_items[2], allowed),
        (query_blocks, key_blocks, value_blocks),
    )
    attn_rows = from_heads(merge_heads(attn_blocks))
    gathered_attn, proj_sum = narrow(attn_rows, w_proj, False)
    resid_mid = inputs_f + proj_sum + shift_proj
    normed_two, inverse_two, ln_two = norm_forward(resid_mid, gain_two, shift_two)
    gathered_two, up_sum = widen(ln_two, w_up, False)
    pre_act = up_sum + up_shift
    activated = gelu_tanh(pre_act).astype(jnp.bfloat16)
    gathered_act, down_sum = narrow(activated, w_down, False)
    block_out = (resid_mid + down_sum + shift_down).astype(jnp.bfloat16)
    grad_top = upstream.astype(jnp.float32)
    gathered_top, grad_act = widen(upstream, w_down, True)
    grad_pre = grad_act * gelu_slope(pre_act)
    grad_pre_half = grad_pre.astype(jnp.bfloat16)
    gathered_pre, grad_ln_two = narrow(grad_pre_half, w_up, True)
    down_part = jnp.dot(gathered_act.T, gathered_top, preferred_element_type=jnp.float32)
    up_part = jnp.dot(gathered_two.T, gathered_pre, preferred_element_type=jnp.float32)
    grad_mid = grad_top + norm_backward(grad_ln_two, normed_two, inverse_two, gain_two)
    grad_mid_half = grad_mid.astype(jnp.bfloat16)
    gathered_mid, grad_attn = widen(grad_mid_half, w_proj, True)
    proj_part = jnp.dot(gathered_attn.T, gathered_mid, preferred_element_type=jnp.float32)
    grad_heads = to_heads(grad_attn.astype(jnp.bfloat16))
    grad_blocks = split_heads(grad_heads)

    def full_pass(block_items):
        query_blk, key_blk, value_blk, log_total, grad_blk = block_items
        chances, grad_scores, grad_query, row_dot = query_side(
            query_blk, key_blk, value_blk, log_total, grad_blk, allowed
        )
        grad_key = (
            jnp.einsum("hqk,hqe->hke", grad_scores, query_blk, preferred_element_type=jnp.float32)
            * factor
        )
        grad_value = jnp.einsum(
            "hqk,hqe->hke",
            chances.astype(jnp.bfloat16),
            grad_blk,
            preferred_element_type=jnp.float32,
        )
        return (grad_query, grad_key, grad_value)

    grad_query_blocks, key_grad_blocks, value_grad_blocks = lax.map(
        full_pass, (query_blocks, key_blocks, value_blocks, log_totals, grad_blocks)
    )
    key_value_grads = jnp.concatenate(
        [merge_heads(key_grad_blocks), merge_heads(value_grad_blocks)], axis=1
    )
    own_kv = lax.psum_scatter(
        key_value_grads.astype(jnp.bfloat16), ("row", "col"), scatter_dimension=0, tiled=True
    ).astype(jnp.float32)
    grad_query_rows = merge_heads(grad_query_blocks)
    bias_query = jnp.sum(grad_query_rows, axis=0)
    bias_value = jnp.sum(own_kv[:, D:], axis=0)
    grad_qkv = jnp.concatenate([grad_query_rows, own_kv], axis=1).astype(jnp.bfloat16)
    gathered_qkv, grad_ln_one = narrow(from_heads(grad_qkv), w_qkv, True)
    qkv_part = jnp.dot(gathered_one.T, gathered_qkv, preferred_element_type=jnp.float32)
    grad_input = grad_mid + norm_backward(grad_ln_one, normed_one, inverse_one, gain_one)
    input_grad = grad_input.astype(jnp.bfloat16)
    vector_part = jnp.stack(
        [
            place_rows(jnp.sum(grad_ln_one * normed_one, axis=0)),
            place_rows(jnp.sum(grad_ln_one, axis=0)),
            bias_query,
            bias_value,
            place_rows(jnp.sum(grad_mid, axis=0)),
            place_rows(jnp.sum(grad_ln_two * normed_two, axis=0)),
            place_rows(jnp.sum(grad_ln_two, axis=0)),
            place_rows(jnp.sum(grad_top, axis=0)),
        ]
    )
    bias_part = lax.dynamic_update_slice_in_dim(
        jnp.zeros((up_bias.shape[0],), jnp.float32),
        jnp.sum(grad_pre, axis=0),
        col_index * up_cols,
        0,
    )
    vector_grad, bias_grad = lax.psum((vector_part, bias_part), ("dp", "row", "col"))
    qkv_grad, proj_grad, up_grad, down_grad = (
        lax.psum_scatter(
            qkv_part.astype(jnp.bfloat16), "dp", scatter_dimension=0, tiled=True
        ).astype(jnp.float32),
        lax.psum_scatter(
            proj_part.astype(jnp.bfloat16), "dp", scatter_dimension=0, tiled=True
        ).astype(jnp.float32),
        lax.psum_scatter(
            up_part.astype(jnp.bfloat16), "dp", scatter_dimension=0, tiled=True
        ).astype(jnp.float32),
        lax.psum_scatter(
            down_part.astype(jnp.bfloat16), "dp", scatter_dimension=0, tiled=True
        ).astype(jnp.float32),
    )
    new_qkv, qkv_state = adam_step(qkv_weight, qkv_grad, qkv_moments, LR_MATRIX)
    new_proj, proj_state = adam_step(proj_weight, proj_grad, proj_moments, LR_MATRIX)
    new_up, up_state = adam_step(up_weight, up_grad, up_moments, LR_MATRIX)
    new_down, down_state = adam_step(down_weight, down_grad, down_moments, LR_MATRIX)
    new_vectors, vector_state = adam_step(vectors, vector_grad, vector_moments, LR_VECTOR)
    new_bias, bias_state = adam_step(up_bias, bias_grad, bias_moments, LR_VECTOR)
    return (
        block_out,
        input_grad,
        qkv_grad,
        proj_grad,
        up_grad,
        down_grad,
        vector_grad,
        bias_grad,
        new_qkv,
        new_proj,
        new_up,
        new_down,
        new_vectors,
        new_bias,
        qkv_state,
        proj_state,
        up_state,
        down_state,
        vector_state,
        bias_state,
    )


def solution(mesh):
    placed = (
        P(("dp", "col"), "row"),
        P(("dp", "col"), "row"),
        P("dp"),
        P(("row", "dp"), "col"),
        P(("col", "dp"), "row"),
        P(("row", "dp"), "col"),
        P(("col", "dp"), "row"),
        P(),
        P(),
        P(None, ("row", "dp"), "col"),
        P(None, ("col", "dp"), "row"),
        P(None, ("row", "dp"), "col"),
        P(None, ("col", "dp"), "row"),
        P(),
        P(),
    )
    return jax.shard_map(
        per_device,
        mesh=mesh,
        in_specs=placed,
        out_specs=(
            P(("dp", "col"), "row"),
            P(("dp", "col"), "row"),
            P(("row", "dp"), "col"),
            P(("col", "dp"), "row"),
            P(("row", "dp"), "col"),
            P(("col", "dp"), "row"),
            P(),
            P(),
            P(("row", "dp"), "col"),
            P(("col", "dp"), "row"),
            P(("row", "dp"), "col"),
            P(("col", "dp"), "row"),
            P(),
            P(),
            P(None, ("row", "dp"), "col"),
            P(None, ("col", "dp"), "row"),
            P(None, ("row", "dp"), "col"),
            P(None, ("col", "dp"), "row"),
            P(),
            P(),
        ),
        check_vma=False,
    )
```

profile of v0, /device:TPU:8, one launch (start us, length us, event | category | flops | bytes accessed | tf_op | source)
XLA Modules:
  0.0 1603.9 jit_solution(6416699591523800499)
XLA Ops:
  10.8 9.0 all-reduce.5
  21.8 12.3 all_gather.40
  49.7 88.4 %reduce-scatter.20.cloned.1.call-done = bf16[512,1200]{0,1:T(8,128)(2,1)} async-done(((bf16[2048,1200]{0,1:T(8,128)(2,1)}), bf16[512,1200]{0,1:T(8,128)(2,1)}) %reduce-scatter.20.cloned.1.call-update) | async-done | bytes 1228816 | tf_op jit(solution)/shard_map/reduce_scatter | solution.py:65
  139.7 18.9 %all_to_all.70 = bf16[4,128,1200]{1,2,0:T(8,128)(2,1)S(1)} all-to-all(bf16[4,128,1200]{1,2,0:T(8,128)(2,1)S(1)} %copy_bitcast_fusion.1), channel_id=1, replica_groups=mesh['dp'=2,'row'=4,'col'=4] {'col'}, dimensions={0} | all-to-all | bytes 2457600 | tf_op jit(solution)/shard_map/all_to_all | solution.py:84
  159.8 105.0 %all-gather.15.cloned.1.call-done = bf16[2048,3200]{0,1:T(8,128)(2,1)} async-done(((bf16[128,3200]{0,1:T(8,128)(2,1)}), bf16[2048,3200]{0,1:T(8,128)(2,1)}) %all-gather.15.cloned.1.call-update) | async-done | bytes 13107216 | tf_op jit(solution)/shard_map/all_gather | solution.py:204
  264.7 11.0 fusion.116
  275.8 36.2 %while.28 = (s32[]{:T(128)}, bf16[5,5,128,64]{2,3,1,0:T(8,128)(2,1)S(1)}, f32[5,5,128,1]{2,1,3,0:T(8,128)S(1)}, bf16[5,5,128,64]{2,3,1,0:T(8,128)(2,1)S(1)}, bf1...) while((s32[]{:T(128)}, ...), condition=%wide.region_8.9_spmd.clone, body=%wide.region_5.8_spmd.clone.sunk | while | flops 350788992 | bytes 19602032 | solution.py:208
  312.0 10.1 all_to_all.71
  330.7 29.5 %all-gather.17.cloned.1.call-done = bf16[2048,400]{0,1:T(8,128)(2,1)} async-done(((bf16[512,400]{0,1:T(8,128)(2,1)}), bf16[2048,400]{0,1:T(8,128)(2,1)}) %all-gather.17.cloned.1.call-update) | async-done | bytes 1638416 | tf_op jit(solution)/shard_map/all_gather | solution.py:72
  369.2 23.3 %reduce-scatter.22.cloned.1.call-done = bf16[512,400]{0,1:T(8,128)(2,1)} async-done(((bf16[2048,400]{0,1:T(8,128)(2,1)}), bf16[512,400]{0,1:T(8,128)(2,1)}) %reduce-scatter.22.cloned.1.call-update) | async-done | bytes 409616 | tf_op jit(solution)/shard_map/reduce_scatter | solution.py:77
  393.7 8.9 all-reduce.4
  421.4 18.1 %all-gather.21.cloned.1.call-done = bf16[400,1600]{1,0:T(8,128)(2,1)} async-done(((bf16[200,1600]{1,0:T(8,128)(2,1)}), bf16[400,1600]{1,0:T(8,128)(2,1)}) %all-gather.21.cloned.1.call-update) | async-done | bytes 1280016 | tf_op jit(solution)/shard_map/all_gather | solution.py:169
  439.5 22.1 %all-gather.19.cloned.1.call-done = bf16[2048,400]{0,1:T(8,128)(2,1)} async-done(((bf16[512,400]{0,1:T(8,128)(2,1)}), bf16[2048,400]{0,1:T(8,128)(2,1)}) %all-gather.19.cloned.1.call-update) | async-done | bytes 1638416 | tf_op jit(solution)/shard_map/all_gather | solution.py:60
  470.7 65.9 %reduce-scatter.28.cloned.1.call-done = bf16[512,1600]{0,1:T(8,128)(2,1)} async-done(((bf16[2048,1600]{0,1:T(8,128)(2,1)}), bf16[512,1600]{0,1:T(8,128)(2,1)}) %reduce-scatter.28.cloned.1.call-update) | async-done | bytes 1638416 | tf_op jit(solution)/shard_map/reduce_scatter | solution.py:65
  536.5 117.9 %reduce-scatter.24.cloned.1.call-done = bf16[512,1600]{0,1:T(8,128)(2,1)} async-done(((bf16[2048,1600]{0,1:T(8,128)(2,1)}), bf16[512,1600]{0,1:T(8,128)(2,1)}) %reduce-scatter.24.cloned.1.call-update) | async-done | bytes 1638416 | tf_op jit(solution)/shard_map/reduce_scatter | solution.py:65
  661.0 116.3 %all-gather.27.cloned.1.call-done = bf16[2048,1600]{0,1:T(8,128)(2,1)} async-done(((bf16[512,1600]{0,1:T(8,128)(2,1)}), bf16[2048,1600]{0,1:T(8,128)(2,1)}) %all-gather.27.cloned.1.call-update) | async-done | bytes 6553616 | tf_op jit(solution)/shard_map/all_gather | solution.py:72
  784.9 112.4 %all-gather.23.cloned.1.call-done = bf16[2048,1600]{0,1:T(8,128)(2,1)} async-done(((bf16[512,1600]{0,1:T(8,128)(2,1)}), bf16[2048,1600]{0,1:T(8,128)(2,1)}) %all-gather.23.cloned.1.call-update) | async-done | bytes 6553616 | tf_op jit(solution)/shard_map/all_gather | solution.py:72
  906.2 11.8 all-reduce.3
  918.1 16.2 %reduce-scatter.26.cloned.1.call-done = bf16[512,400]{0,1:T(8,128)(2,1)} async-done(((bf16[2048,400]{0,1:T(8,128)(2,1)}), bf16[512,400]{0,1:T(8,128)(2,1)}) %reduce-scatter.26.cloned.1.call-update) | async-done | bytes 409616 | tf_op jit(solution)/shard_map/reduce_scatter | solution.py:77
  938.3 19.9 %all-gather.29.cloned.1.call-done = bf16[2048,400]{0,1:T(8,128)(2,1)} async-done(((bf16[512,400]{0,1:T(8,128)(2,1)}), bf16[2048,400]{0,1:T(8,128)(2,1)}) %all-gather.29.cloned.1.call-update) | async-done | bytes 1638416 | tf_op jit(solution)/shard_map/all_gather | solution.py:60
  961.8 35.5 %reduce-scatter.32.cloned.1.call-done = bf16[512,400]{0,1:T(8,128)(2,1)} async-done(((bf16[2048,400]{0,1:T(8,128)(2,1)}), bf16[512,400]{0,1:T(8,128)(2,1)}) %reduce-scatter.32.cloned.1.call-update) | async-done | bytes 409616 | tf_op jit(solution)/shard_map/reduce_scatter | solution.py:65
  1010.2 61.5 %while.29 = (s32[]{:T(128)}, f32[5,5,128,64]{2,3,1,0:T(8,128)S(1)}, bf16[5,5,2048,64]{2,3,1,0:T(8,128)(2,1)}, bf16[5,5,2048,64]{2,3,1,0:T(8,128)(2,1)}, bf16[5,5...) while((s32[]{:T(128)}, f32[5,5,128,64]{2,3,1,0:T(8,128)S(1)}, ...), condition=%wide.region_25.26_spmd.clone, body=%wide.region_23.25_spmd.clone.sunk | while | flops 852139392 | bytes 49541256 | solution.py:252
  1071.7 10.3 pad_maximum_fusion
  1082.0 17.3 %copy.50 = bf16[2048,3200]{1,0:T(8,128)(2,1)} copy(bf16[2048,3200]{0,1:T(8,128)(2,1)} %pad_maximum_fusion) | data formatting | bytes 26214400
  1111.8 124.4 %reduce-scatter.40.cloned.1.call-done = bf16[128,3200]{1,0:T(8,128)(2,1)} async-done(((bf16[2048,3200]{1,0:T(8,128)(2,1)}), bf16[128,3200]{1,0:T(8,128)(2,1)}) %reduce-scatter.40.cloned.1.call-update) | async-done | bytes 819216
  1239.0 18.9 %all_to_all.72 = bf16[128,4,1200]{0,2,1:T(8,128)(2,1)S(1)} all-to-all(bf16[128,4,1200]{0,2,1:T(8,128)(2,1)S(1)} %bitcast.304), channel_id=1, replica_groups=mesh['dp'=2,'row'=4,'col'=4] {'col'}, dimensions={1} | all-to-all | bytes 2457600 | tf_op jit(solution)/shard_map/all_to_all | solution.py:88
  1274.0 83.8 %all-gather.31.cloned.1.call-done = bf16[2048,1200]{0,1:T(8,128)(2,1)} async-done(((bf16[512,1200]{0,1:T(8,128)(2,1)}), bf16[2048,1200]{0,1:T(8,128)(2,1)}) %all-gather.31.cloned.1.call-update) | async-done | bytes 4915216 | tf_op jit(solution)/shard_map/all_gather | solution.py:72
  1370.8 14.7 reduce-scatter.44.cloned.1.call-done
  1408.0 16.4 %reduce-scatter.36.cloned.1.call-done = bf16[200,1200]{1,0:T(8,128)(2,1)} async-done(((bf16[400,1200]{1,0:T(8,128)(2,1)}), bf16[200,1200]{1,0:T(8,128)(2,1)}) %reduce-scatter.36.cloned.1.call-update) | async-done | bytes 480016 | tf_op jit(solution)/shard_map/reduce_scatter | solution.py:289
  1429.4 26.0 %reduce-scatter.34.cloned.1.call-done = bf16[512,400]{0,1:T(8,128)(2,1)} async-done(((bf16[2048,400]{0,1:T(8,128)(2,1)}), bf16[512,400]{0,1:T(8,128)(2,1)}) %reduce-scatter.34.cloned.1.call-update) | async-done | bytes 409616 | tf_op jit(solution)/shard_map/reduce_scatter | solution.py:77
  1456.9 8.9 all-reduce.2
  1469.3 120.2 %all-reduce.8.cloned.1.call-done = (f32[8,1600]{1,0:T(8,128)}, f32[6400]{0:T(1024)}) async-done(((f32[8,1600]{1,0:T(8,128)}, f32[6400]{0:T(1024)}), (f32[8,1600]{1,0:T(8,128)}, f32[6400]{0:T(1024)})) %all-reduce.8.cloned.1.call-update) | async-done | bytes 76816 | tf_op jit(solution)/shard_map/psum | solution.py:287
  (310 shorter events, 293.8 us)
Async XLA Ops:
  8.0 35.0 %all-gather.13.cloned.1.call-start = ((), (), s32[]{:S(2)}) async-start(), calls=%async_computation.17 | async-start | bytes 2048000 | tf_op jit(solution)/shard_map/all_gather | solution.py:60
  21.7 116.4 %reduce-scatter.20.cloned.1.call-start = ((), (), s32[]{:S(2)}) async-start(), calls=%async_computation.18 | async-start | bytes 6144000 | tf_op jit(solution)/shard_map/reduce_scatter | solution.py:65
  49.5 215.3 %all-gather.15.cloned.1.call-start = ((), (), s32[]{:S(2)}) async-start(), calls=%async_computation.19 | async-start | bytes 13926400 | tf_op jit(solution)/shard_map/all_gather | solution.py:204
  159.6 200.6 %all-gather.17.cloned.1.call-start = ((), (), s32[]{:S(2)}) async-start(), calls=%async_computation.20 | async-start | bytes 2048000 | tf_op jit(solution)/shard_map/all_gather | solution.py:72
  322.9 69.6 %reduce-scatter.22.cloned.1.call-start = ((), (), s32[]{:S(2)}) async-start(), calls=%async_computation.21 | async-start | bytes 2048000 | tf_op jit(solution)/shard_map/reduce_scatter | solution.py:77
  363.8 41.1 %all-gather.33.cloned.1.call-start = ((), (), s32[]{:S(2)}) async-start(), calls=%async_computation.37 | async-start | bytes 2150400 | tf_op jit(solution)/shard_map/all_gather | solution.py:170
  366.1 47.1 %all-gather.25.cloned.1.call-start = ((), (), s32[]{:S(2)}) async-start(), calls=%async_computation.27 | async-start | bytes 2048000 | tf_op jit(solution)/shard_map/all_gather | solution.py:60
  366.7 72.8 %all-gather.21.cloned.1.call-start = ((), (), s32[]{:S(2)}) async-start(), calls=%async_computation.23 | async-start | bytes 1996800 | tf_op jit(solution)/shard_map/all_gather | solution.py:169
  369.0 92.6 %all-gather.19.cloned.1.call-start = ((), (), s32[]{:S(2)}) async-start(), calls=%async_computation.22 | async-start | bytes 2048000 | tf_op jit(solution)/shard_map/all_gather | solution.py:60
  404.7 131.8 %reduce-scatter.28.cloned.1.call-start = ((), (), s32[]{:S(2)}) async-start(), calls=%async_computation.28 | async-start | bytes 8192000 | tf_op jit(solution)/shard_map/reduce_scatter | solution.py:65
  421.4 233.0 %reduce-scatter.24.cloned.1.call-start = ((), (), s32[]{:S(2)}) async-start(), calls=%async_computation.24 | async-start | bytes 8192000 | tf_op jit(solution)/shard_map/reduce_scatter | solution.py:65
  469.8 307.4 %all-gather.27.cloned.1.call-start = ((), (), s32[]{:S(2)}) async-start(), calls=%async_computation.29 | async-start | bytes 8192000 | tf_op jit(solution)/shard_map/all_gather | solution.py:72
  659.9 237.4 %all-gather.23.cloned.1.call-start = ((), (), s32[]{:S(2)}) async-start(), calls=%async_computation.25 | async-start | bytes 8192000 | tf_op jit(solution)/shard_map/all_gather | solution.py:72
  660.7 236.7 %copy-start.19 = (bf16[1600,400]{0,1:T(8,128)(2,1)S(1)}, bf16[1600,400]{0,1:T(8,128)(2,1)}, u32[]{:S(2)}) copy-start(bf16[1600,400]{0,1:T(8,128)(2,1)} %reshape.176) | copy-start | bytes 3840004
  660.7 243.9 %reduce-scatter.30.cloned.1.call-start = ((), (), s32[]{:S(2)}) async-start(), calls=%async_computation.30 | async-start | bytes 2048000 | tf_op jit(solution)/shard_map/reduce_scatter | solution.py:77
  784.8 119.7 %copy-start.1 = (bf16[512,400]{0,1:T(8,128)(2,1)S(1)}, bf16[512,400]{0,1:T(8,128)(2,1)}, u32[]{:S(2)}) copy-start(bf16[512,400]{0,1:T(8,128)(2,1)} %reduce-scatter.22.cloned.1.call-done) | copy-start | bytes 1228804
  784.9 149.4 %reduce-scatter.26.cloned.1.call-start = ((), (), s32[]{:S(2)}) async-start(), calls=%async_computation.26 | async-start | bytes 2048000 | tf_op jit(solution)/shard_map/reduce_scatter | solution.py:77
  904.5 53.8 %all-gather.29.cloned.1.call-start = ((), (), s32[]{:S(2)}) async-start(), calls=%async_computation.31 | async-start | bytes 2048000 | tf_op jit(solution)/shard_map/all_gather | solution.py:60
  938.2 59.1 %reduce-scatter.32.cloned.1.call-start = ((), (), s32[]{:S(2)}) async-start(), calls=%async_computation.32 | async-start | bytes 2048000 | tf_op jit(solution)/shard_map/reduce_scatter | solution.py:65
  999.1 11.1 all-to-all-start.2
  1002.6 233.6 %reduce-scatter.40.cloned.1.call-start = ((), (), s32[]{:S(2)}) async-start(), calls=%async_computation.38 | async-start | bytes 13926400
  1099.3 168.6 %reduce-scatter.42.cloned.1.call-start = ((), (), s32[]{:S(2)}) async-start(), calls=%async_computation.39 | async-start | bytes 2457600
  1110.9 246.9 %all-gather.31.cloned.1.call-start = ((), (), s32[]{:S(2)}) async-start(), calls=%async_computation.33 | async-start | bytes 6144000 | tf_op jit(solution)/shard_map/all_gather | solution.py:72
  1259.1 126.4 %reduce-scatter.44.cloned.1.call-start = ((), (), s32[]{:S(2)}) async-start(), calls=%async_computation.40 | async-start | bytes 1996800
  1266.8 135.6 %reduce-scatter.38.cloned.1.call-start = ((), (), s32[]{:S(2)}) async-start(), calls=%async_computation.36 | async-start | bytes 614400 | tf_op jit(solution)/shard_map/reduce_scatter | solution.py:292
  1273.9 150.5 %reduce-scatter.36.cloned.1.call-start = ((), (), s32[]{:S(2)}) async-start(), calls=%async_computation.35 | async-start | bytes 1536000 | tf_op jit(solution)/shard_map/reduce_scatter | solution.py:289
  1364.0 91.5 %reduce-scatter.34.cloned.1.call-start = ((), (), s32[]{:S(2)}) async-start(), calls=%async_computation.34 | async-start | bytes 2048000 | tf_op jit(solution)/shard_map/reduce_scatter | solution.py:77
  1394.9 194.6 %all-reduce.8.cloned.1.call-start = ((), (), s32[]{:S(2)}) async-start(), calls=%async_computation.41 | async-start | bytes 163840 | tf_op jit(solution)/shard_map/psum | solution.py:287
  1429.4 160.1 %copy-start.27 = (f32[6400]{0:T(1024)S(1)}, f32[6400]{0:T(1024)}, u32[]{:S(2)}) copy-start(f32[6400]{0:T(1024)} %get-tuple-element.184) | copy-start | bytes 76804
  1429.4 160.1 %copy-start.30 = (f32[6400]{0:T(1024)S(1)}, f32[6400]{0:T(1024)}, u32[]{:S(2)}) copy-start(f32[6400]{0:T(1024)} %param.27) | copy-start | bytes 76804
  1429.4 162.2 %copy-start.25 = (f32[8,1600]{1,0:T(8,128)S(1)}, f32[8,1600]{1,0:T(8,128)}, u32[]{:S(2)}) copy-start(f32[8,1600]{1,0:T(8,128)} %param.26) | copy-start | bytes 153604
  1429.4 162.2 %copy-start.28 = (f32[2,8,1600]{2,1,0:T(8,128)S(1)}, f32[2,8,1600]{2,1,0:T(8,128)}, u32[]{:S(2)}) copy-start(f32[2,8,1600]{2,1,0:T(8,128)} %param.32) | copy-start | bytes 307204
  (36 other events, 506.1 us)
Sparse Core Ops, SparseCore 0:
  21.8 21.1 all-gather.12
  49.6 88.4 reduce-scatter.19
  159.7 104.9 all-gather.14
  323.0 37.1 all-gather.16
  363.9 28.5 reduce-scatter.21
  421.5 115.0 reduce-scatter.27
  538.8 115.5 reduce-scatter.23
  660.1 117.1 all-gather.26
  779.5 117.8 all-gather.22
  962.0 35.2 reduce-scatter.31
  1099.4 136.7 reduce-scatter.39
  1238.9 26.7 reduce-scatter.41
  1267.9 89.8 all-gather.30
  1360.5 24.9 reduce-scatter.43
  1388.3 13.3 reduce-scatter.37
  1404.3 20.0 reduce-scatter.35
  1426.8 28.5 reduce-scatter.33
Sparse Core Ops, SparseCore 1:
  366.4 25.4 all-gather.32
  393.3 19.8 all-gather.24
  415.2 24.3 all-gather.20
  441.7 19.9 all-gather.18
  784.9 29.7 reduce-scatter.29
  904.5 29.7 reduce-scatter.25
  938.3 19.8 all-gather.28
  1467.3 122.2 all-reduce.7
where the time goes:
time: 1610 us; the launch traced here: 1600 us
  waiting for transfers between devices  1180 us (73%)
  matrix products  160 us (10%)
  blocking collectives  107 us (7%)
  other arithmetic  81.7 us (5%)
  local copies, waits for them, and re-layouts  56.1 us (3%)
  between operations  16.4 us (1%)
    all_gather x4, waiting for transfers between devices, narrow(): gathered = lax.all_gather(local_rows, 'row', axis=0, tiled=True)  342 us
    reduce_scatter x4, waiting for transfers between devices, widen(): lax.psum_scatter(partial_rows.astype(jnp.bfloat16), 'row', scatter_dimens...  308 us
    unnamed x28, waiting for transfers between devices  141 us
    psum x1, waiting for transfers between devices, per_device(): lax.psum((vector_part, bias_part), ('dp', 'row', 'col'))  120 us
    all_gather x1, waiting for transfers between devices, per_device(): lax.all_gather(qkv_heads[:, D:], ('row', 'col'), axis=0, tiled=True)  105 us
    reduce_scatter x4, waiting for transfers between devices, narrow(): lax.psum_scatter(partial_rows.astype(jnp.bfloat16), 'col', scatter_dimens...  65.5 us
    all_gather x4, waiting for transfers between devices, widen(): gathered = lax.all_gather(local_rows, 'col', axis=0, tiled=True)  54.8 us
    psum x4, blocking collectives, row_totals(): lax.psum((jnp.sum(first_term, axis=1, keepdims=True), jnp.sum(second_term...  38.6 us
  transfers between devices with their start and end apart: 26, of which 22 were waited for; matrix products, arithmetic and copies ran while one was open for 7% of the time, Pallas kernels for 0%

commit v1 on v0

--- a/solution.py
+++ b/solution.py
@@ -57,7 +57,14 @@
 
 
 def widen(local_rows, weight_block, flipped):
-    gathered = lax.all_gather(local_rows, "col", axis=0, tiled=True)
+    x = local_rows
+    ways, here, lap = (lax.axis_size("col"), lax.axis_index("col"), x.shape[0])
+    shape = [n * ways if d == 0 else n for d, n in enumerate(x.shape)]
+    full = lax.dynamic_update_slice_in_dim(jnp.zeros(shape, x.dtype), x, here * lap, axis=0)
+    for far in range(1, ways):
+        x = lax.ppermute(x, "col", [(d, (d + 1) % ways) for d in range(ways)])
+        full = lax.dynamic_update_slice_in_dim(full, x, (here - far) % ways * lap, axis=0)
+    gathered = full
     right_side = weight_block.T if flipped else weight_block
     partial_rows = jnp.dot(gathered, right_side, preferred_element_type=jnp.float32)
     return (

time: 1610 us -> 1680 us (1.043)
  waiting for transfers between devices: 1180 us -> 1240 us
    ppermute x0 -> x12, waiting for transfers between devices: none -> 74.6 us  [widen(): x = lax.ppermute(x, 'col', [(d, (d + 1) % ways) for d in range(ways)])]
    all_gather x4 -> x0, waiting for transfers between devices: 54.8 us -> none  [widen(): gathered = lax.all_gather(local_rows, 'col', axis=0, tiled=True)]
    reduce_scatter x4, waiting for transfers between devices: 308 us -> 342 us  [widen(): lax.psum_scatter(partial_rows.astype(jnp.bfloat16), 'row', scatter_dimens...]
    reduce_scatter x4, waiting for transfers between devices: 65.5 us -> 90.3 us  [narrow(): lax.psum_scatter(partial_rows.astype(jnp.bfloat16), 'col', scatter_dimens...]
    all_gather x1, waiting for transfers between devices: 18.1 us -> 0.01 us  [per_device(): lax.all_gather(up_weight.astype(jnp.bfloat16), 'dp', axis=0, tiled=True)]
    unnamed x28 -> x24, waiting for transfers between devices: 141 us -> 140 us
  transfers between devices with their start and end apart: 26 -> 34, of which waited for: 22 -> 30; matrix products, arithmetic and copies ran while one was open for 7% -> 8% of each run, Pallas kernels for 0% -> 0%
where the time goes in v1:
time: 1680 us; the launch traced here: 1670 us
  waiting for transfers between devices  1240 us (74%)
  matrix products  159 us (9%)
  blocking collectives  106 us (6%)
  other arithmetic  76.4 us (5%)
  local copies, waits for them, and re-layouts  68.2 us (4%)
    reduce_scatter x4, waiting for transfers between devices, widen(): lax.psum_scatter(partial_rows.astype(jnp.bfloat16), 'row', scatter_dimens...  342 us
    all_gather x4, waiting for transfers between devices, narrow(): gathered = lax.all_gather(local_rows, 'row', axis=0, tiled=True)  340 us
    unnamed x24, waiting for transfers between devices  140 us
    psum x1, waiting for transfers between devices, per_device(): lax.psum((vector_part, bias_part), ('dp', 'row', 'col'))  121 us
    all_gather x1, waiting for transfers between devices, per_device(): lax.all_gather(qkv_heads[:, D:], ('row', 'col'), axis=0, tiled=True)  105 us
    reduce_scatter x4, waiting for transfers between devices, narrow(): lax.psum_scatter(partial_rows.astype(jnp.bfloat16), 'col', scatter_dimens...  90.3 us
    ppermute x12, waiting for transfers between devices, widen(): x = lax.ppermute(x, 'col', [(d, (d + 1) % ways) for d in range(ways)])  74.6 us
    psum x4, blocking collectives, row_totals(): lax.psum((jnp.sum(first_term, axis=1, keepdims=True), jnp.sum(second_term...  35.7 us
  transfers between devices with their start and end apart: 34, of which 30 were waited for; matrix products, arithmetic and copies ran while one was open for 8% of the time, Pallas kernels for 0%

profile of v1, /device:TPU:8, one launch (start us, length us, event | category | flops | bytes accessed | tf_op | source)
XLA Modules:
  0.0 1669.2 jit_solution(7129479096504234586)
XLA Ops:
  9.9 9.0 all-reduce.5
  36.0 14.6 all_gather.27
  59.6 89.8 %reduce-scatter.20.cloned.1.call-done = bf16[512,1200]{0,1:T(8,128)(2,1)} async-done(((bf16[2048,1200]{0,1:T(8,128)(2,1)}), bf16[512,1200]{0,1:T(8,128)(2,1)}) %reduce-scatter.20.cloned.1.call-update) | async-done | bytes 1228816 | tf_op jit(solution)/shard_map/reduce_scatter | solution.py:72
  151.0 18.9 %all_to_all.70 = bf16[4,128,1200]{1,2,0:T(8,128)(2,1)S(1)} all-to-all(bf16[4,128,1200]{1,2,0:T(8,128)(2,1)S(1)} %copy_bitcast_fusion.1), channel_id=1, replica_groups=mesh['dp'=2,'row'=4,'col'=4] {'col'}, dimensions={0} | all-to-all | bytes 2457600 | tf_op jit(solution)/shard_map/all_to_all | solution.py:91
  171.1 104.9 %all-gather.9.cloned.1.call-done = bf16[2048,3200]{0,1:T(8,128)(2,1)} async-done(((bf16[128,3200]{0,1:T(8,128)(2,1)}), bf16[2048,3200]{0,1:T(8,128)(2,1)}) %all-gather.9.cloned.1.call-update) | async-done | bytes 13107216 | tf_op jit(solution)/shard_map/all_gather | solution.py:211
  276.0 11.0 fusion.117
  287.1 36.1 %while.28 = (s32[]{:T(128)}, bf16[5,5,128,64]{2,3,1,0:T(8,128)(2,1)S(1)}, f32[5,5,128,1]{2,1,3,0:T(8,128)S(1)}, bf16[5,5,128,64]{2,3,1,0:T(8,128)(2,1)S(1)}, bf1...) while((s32[]{:T(128)}, ...), condition=%wide.region_8.9_spmd.clone, body=%wide.region_5.8_spmd.clone.sunk | while | flops 350788992 | bytes 19602032 | solution.py:215
  323.2 10.1 all_to_all.71
  342.9 28.5 %all-gather.11.cloned.1.call-done = bf16[2048,400]{0,1:T(8,128)(2,1)} async-done(((bf16[512,400]{0,1:T(8,128)(2,1)}), bf16[2048,400]{0,1:T(8,128)(2,1)}) %all-gather.11.cloned.1.call-update) | async-done | bytes 1638416 | tf_op jit(solution)/shard_map/all_gather | solution.py:79
  403.3 8.2 convolution_convert_fusion
  411.7 19.0 %reduce-scatter.22.cloned.1.call-done = bf16[512,400]{0,1:T(8,128)(2,1)} async-done(((bf16[2048,400]{0,1:T(8,128)(2,1)}), bf16[512,400]{0,1:T(8,128)(2,1)}) %reduce-scatter.22.cloned.1.call-update) | async-done | bytes 409616 | tf_op jit(solution)/shard_map/reduce_scatter | solution.py:84
  432.1 8.9 all-reduce.4
  466.3 8.7 convolution_convert_fusion.1
  475.8 98.8 %reduce-scatter.28.cloned.1.call-done = bf16[512,1600]{0,1:T(8,128)(2,1)} async-done(((bf16[2048,1600]{0,1:T(8,128)(2,1)}), bf16[512,1600]{0,1:T(8,128)(2,1)}) %reduce-scatter.28.cloned.1.call-update) | async-done | bytes 1638416 | tf_op jit(solution)/shard_map/reduce_scatter | solution.py:72
  574.6 117.8 %reduce-scatter.24.cloned.1.call-done = bf16[512,1600]{0,1:T(8,128)(2,1)} async-done(((bf16[2048,1600]{0,1:T(8,128)(2,1)}), bf16[512,1600]{0,1:T(8,128)(2,1)}) %reduce-scatter.24.cloned.1.call-update) | async-done | bytes 1638416 | tf_op jit(solution)/shard_map/reduce_scatter | solution.py:72
  699.1 116.3 %all-gather.17.cloned.1.call-done = bf16[2048,1600]{0,1:T(8,128)(2,1)} async-done(((bf16[512,1600]{0,1:T(8,128)(2,1)}), bf16[2048,1600]{0,1:T(8,128)(2,1)}) %all-gather.17.cloned.1.call-update) | async-done | bytes 6553616 | tf_op jit(solution)/shard_map/all_gather | solution.py:79
  823.1 111.6 %all-gather.15.cloned.1.call-done = bf16[2048,1600]{0,1:T(8,128)(2,1)} async-done(((bf16[512,1600]{0,1:T(8,128)(2,1)}), bf16[2048,1600]{0,1:T(8,128)(2,1)}) %all-gather.15.cloned.1.call-update) | async-done | bytes 6553616 | tf_op jit(solution)/shard_map/all_gather | solution.py:79
  942.4 24.6 %reduce-scatter.30.cloned.1.call-done = bf16[512,400]{0,1:T(8,128)(2,1)} async-done(((bf16[2048,400]{0,1:T(8,128)(2,1)}), bf16[512,400]{0,1:T(8,128)(2,1)}) %reduce-scatter.30.cloned.1.call-update) | async-done | bytes 409616 | tf_op jit(solution)/shard_map/reduce_scatter | solution.py:84
  968.6 8.9 all-reduce.3
  977.5 20.7 %reduce-scatter.26.cloned.1.call-done = bf16[512,400]{0,1:T(8,128)(2,1)} async-done(((bf16[2048,400]{0,1:T(8,128)(2,1)}), bf16[512,400]{0,1:T(8,128)(2,1)}) %reduce-scatter.26.cloned.1.call-update) | async-done | bytes 409616 | tf_op jit(solution)/shard_map/reduce_scatter | solution.py:84
  1027.3 35.5 %reduce-scatter.32.cloned.1.call-done = bf16[512,400]{0,1:T(8,128)(2,1)} async-done(((bf16[2048,400]{0,1:T(8,128)(2,1)}), bf16[512,400]{0,1:T(8,128)(2,1)}) %reduce-scatter.32.cloned.1.call-update) | async-done | bytes 409616 | tf_op jit(solution)/shard_map/reduce_scatter | solution.py:72
  1075.6 61.5 %while.29 = (s32[]{:T(128)}, f32[5,5,128,64]{2,3,1,0:T(8,128)S(1)}, bf16[5,5,2048,64]{2,3,1,0:T(8,128)(2,1)}, bf16[5,5,2048,64]{2,3,1,0:T(8,128)(2,1)}, bf16[5,5...) while((s32[]{:T(128)}, f32[5,5,128,64]{2,3,1,0:T(8,128)S(1)}, ...), condition=%wide.region_25.26_spmd.clone, body=%wide.region_23.25_spmd.clone.sunk | while | flops 852139392 | bytes 49541256 | solution.py:259
  1137.1 10.3 pad_maximum_fusion
  1147.5 16.9 %copy.50 = bf16[2048,3200]{1,0:T(8,128)(2,1)} copy(bf16[2048,3200]{0,1:T(8,128)(2,1)} %pad_maximum_fusion) | data formatting | bytes 26214400
  1176.5 124.6 %reduce-scatter.40.cloned.1.call-done = bf16[128,3200]{1,0:T(8,128)(2,1)} async-done(((bf16[2048,3200]{1,0:T(8,128)(2,1)}), bf16[128,3200]{1,0:T(8,128)(2,1)}) %reduce-scatter.40.cloned.1.call-update) | async-done | bytes 819216
  1304.0 18.9 %all_to_all.72 = bf16[128,4,1200]{0,2,1:T(8,128)(2,1)S(1)} all-to-all(bf16[128,4,1200]{0,2,1:T(8,128)(2,1)S(1)} %bitcast.304), channel_id=1, replica_groups=mesh['dp'=2,'row'=4,'col'=4] {'col'}, dimensions={1} | all-to-all | bytes 2457600 | tf_op jit(solution)/shard_map/all_to_all | solution.py:95
  1339.2 83.4 %all-gather.19.cloned.1.call-done = bf16[2048,1200]{0,1:T(8,128)(2,1)} async-done(((bf16[512,1200]{0,1:T(8,128)(2,1)}), bf16[2048,1200]{0,1:T(8,128)(2,1)}) %all-gather.19.cloned.1.call-update) | async-done | bytes 4915216 | tf_op jit(solution)/shard_map/all_gather | solution.py:79
  1435.6 14.7 reduce-scatter.44.cloned.1.call-done
  1472.0 17.4 %reduce-scatter.36.cloned.1.call-done = bf16[200,1200]{1,0:T(8,128)(2,1)} async-done(((bf16[400,1200]{1,0:T(8,128)(2,1)}), bf16[200,1200]{1,0:T(8,128)(2,1)}) %reduce-scatter.36.cloned.1.call-update) | async-done | bytes 480016 | tf_op jit(solution)/shard_map/reduce_scatter | solution.py:296
  1494.4 26.0 %reduce-scatter.34.cloned.1.call-done = bf16[512,400]{0,1:T(8,128)(2,1)} async-done(((bf16[2048,400]{0,1:T(8,128)(2,1)}), bf16[512,400]{0,1:T(8,128)(2,1)}) %reduce-scatter.34.cloned.1.call-update) | async-done | bytes 409616 | tf_op jit(solution)/shard_map/reduce_scatter | solution.py:84
  1521.8 8.9 all-reduce.2
  1534.2 120.6 %all-reduce.8.cloned.1.call-done = (f32[8,1600]{1,0:T(8,128)}, f32[6400]{0:T(1024)}) async-done(((f32[8,1600]{1,0:T(8,128)}, f32[6400]{0:T(1024)}), (f32[8,1600]{1,0:T(8,128)}, f32[6400]{0:T(1024)})) %all-reduce.8.cloned.1.call-update) | async-done | bytes 76816 | tf_op jit(solution)/shard_map/psum | solution.py:294
  (343 shorter events, 345.7 us)
Async XLA Ops:
  7.2 142.2 %reduce-scatter.20.cloned.1.call-start = ((), (), s32[]{:S(2)}) async-start(), calls=%async_computation.17 | async-start | bytes 6144000 | tf_op jit(solution)/shard_map/reduce_scatter | solution.py:72
  21.2 7.4 collective-permute-start
  28.6 7.4 collective-permute-start.1
  36.0 16.2 collective-permute-start.2
  59.4 216.6 %all-gather.9.cloned.1.call-start = ((), (), s32[]{:S(2)}) async-start(), calls=%async_computation.18 | async-start | bytes 13926400 | tf_op jit(solution)/shard_map/all_gather | solution.py:211
  170.9 200.5 %all-gather.11.cloned.1.call-start = ((), (), s32[]{:S(2)}) async-start(), calls=%async_computation.19 | async-start | bytes 2048000 | tf_op jit(solution)/shard_map/all_gather | solution.py:79
  334.1 64.9 %all-gather.21.cloned.1.call-start = ((), (), s32[]{:S(2)}) async-start(), calls=%async_computation.33 | async-start | bytes 2150400 | tf_op jit(solution)/shard_map/all_gather | solution.py:177
  335.1 95.7 %reduce-scatter.22.cloned.1.call-start = ((), (), s32[]{:S(2)}) async-start(), calls=%async_computation.20 | async-start | bytes 2048000 | tf_op jit(solution)/shard_map/reduce_scatter | solution.py:84
  375.1 91.2 %all-gather.13.cloned.1.call-start = ((), (), s32[]{:S(2)}) async-start(), calls=%async_computation.21 | async-start | bytes 1996800 | tf_op jit(solution)/shard_map/all_gather | solution.py:176
  375.2 7.4 collective-permute-start.6
  382.6 7.4 collective-permute-start.7
  383.6 191.1 %reduce-scatter.28.cloned.1.call-start = ((), (), s32[]{:S(2)}) async-start(), calls=%async_computation.25 | async-start | bytes 8192000 | tf_op jit(solution)/shard_map/reduce_scatter | solution.py:72
  390.0 7.6 collective-permute-start.8
  411.5 280.9 %reduce-scatter.24.cloned.1.call-start = ((), (), s32[]{:S(2)}) async-start(), calls=%async_computation.22 | async-start | bytes 8192000 | tf_op jit(solution)/shard_map/reduce_scatter | solution.py:72
  443.4 7.4 collective-permute-start.3
  450.8 7.4 collective-permute-start.4
  458.1 7.4 collective-permute-start.5
  475.0 340.4 %all-gather.17.cloned.1.call-start = ((), (), s32[]{:S(2)}) async-start(), calls=%async_computation.26 | async-start | bytes 8192000 | tf_op jit(solution)/shard_map/all_gather | solution.py:79
  698.1 236.6 %all-gather.15.cloned.1.call-start = ((), (), s32[]{:S(2)}) async-start(), calls=%async_computation.23 | async-start | bytes 8192000 | tf_op jit(solution)/shard_map/all_gather | solution.py:79
  698.7 268.4 %reduce-scatter.30.cloned.1.call-start = ((), (), s32[]{:S(2)}) async-start(), calls=%async_computation.27 | async-start | bytes 2048000 | tf_op jit(solution)/shard_map/reduce_scatter | solution.py:84
  823.0 175.2 %reduce-scatter.26.cloned.1.call-start = ((), (), s32[]{:S(2)}) async-start(), calls=%async_computation.24 | async-start | bytes 2048000 | tf_op jit(solution)/shard_map/reduce_scatter | solution.py:84
  942.3 120.4 %reduce-scatter.32.cloned.1.call-start = ((), (), s32[]{:S(2)}) async-start(), calls=%async_computation.28 | async-start | bytes 2048000 | tf_op jit(solution)/shard_map/reduce_scatter | solution.py:72
  1001.6 7.4 collective-permute-start.9
  1064.6 11.1 all-to-all-start.2
  1068.0 233.1 %reduce-scatter.40.cloned.1.call-start = ((), (), s32[]{:S(2)}) async-start(), calls=%async_computation.34 | async-start | bytes 13926400
  1164.4 168.7 %reduce-scatter.42.cloned.1.call-start = ((), (), s32[]{:S(2)}) async-start(), calls=%async_computation.35 | async-start | bytes 2457600
  1175.6 247.0 %all-gather.19.cloned.1.call-start = ((), (), s32[]{:S(2)}) async-start(), calls=%async_computation.29 | async-start | bytes 6144000 | tf_op jit(solution)/shard_map/all_gather | solution.py:79
  1324.1 126.3 %reduce-scatter.44.cloned.1.call-start = ((), (), s32[]{:S(2)}) async-start(), calls=%async_computation.36 | async-start | bytes 1996800
  1331.8 135.7 %reduce-scatter.38.cloned.1.call-start = ((), (), s32[]{:S(2)}) async-start(), calls=%async_computation.32 | async-start | bytes 614400 | tf_op jit(solution)/shard_map/reduce_scatter | solution.py:299
  1339.1 150.3 %reduce-scatter.36.cloned.1.call-start = ((), (), s32[]{:S(2)}) async-start(), calls=%async_computation.31 | async-start | bytes 1536000 | tf_op jit(solution)/shard_map/reduce_scatter | solution.py:296
  1428.8 91.6 %reduce-scatter.34.cloned.1.call-start = ((), (), s32[]{:S(2)}) async-start(), calls=%async_computation.30 | async-start | bytes 2048000 | tf_op jit(solution)/shard_map/reduce_scatter | solution.py:84
  1459.7 195.2 %all-reduce.8.cloned.1.call-start = ((), (), s32[]{:S(2)}) async-start(), calls=%async_computation.37 | async-start | bytes 163840 | tf_op jit(solution)/shard_map/psum | solution.py:294
  (46 other events, 1103.5 us)
Sparse Core Ops, SparseCore 0:
  59.5 89.8 reduce-scatter.19
  171.0 104.9 all-gather.8
  334.2 37.1 all-gather.10
  373.4 25.5 all-gather.20
  402.2 28.5 reduce-scatter.21
  432.8 24.4 all-gather.12
  459.6 115.0 reduce-scatter.27
  576.9 115.4 reduce-scatter.23
  698.2 117.1 all-gather.16
  816.8 117.8 all-gather.14
  937.2 29.7 reduce-scatter.29
  969.6 28.5 reduce-scatter.25
  1027.4 35.2 reduce-scatter.31
  1164.5 136.6 reduce-scatter.39
  1303.8 26.7 reduce-scatter.41
  1332.7 89.8 all-gather.18
  1425.4 24.9 reduce-scatter.43
  1453.1 13.3 reduce-scatter.37
  1469.3 20.0 reduce-scatter.35
  1491.8 28.5 reduce-scatter.33
  1532.3 122.5 all-reduce.7
